TPU v7x, 32 devices: a whole 2x2x4 slice. The times are simulated.
32 devices in a mesh: ue: 8 (over z, y), cell: 4 (over x, core).
Axes of the slice: x: 2, y: 2, z: 4, core: 2. Of those that a mesh axis runs over, the one named last changes fastest.
Arguments:
- gains: bfloat16 [512, 16, 128, 128], P('ue', 'cell'), may hold values from 0 to 4.8828125
- near_blocks: int32 [512, 16], P('ue', 'cell'), may hold values from 0 to 31, as said below
- serve_block: int32 [65536, 1], P(('ue', 'cell')), may hold values from 0 to 31; in each aligned block of 2048 rows (0 to 2047, 2048 to 4095, ...) at most 192 rows name the same one
- serve_cell: int32 [65536], P(('ue', 'cell')), may hold values from 0 to 127
- serve_gain: float32 [65536], P(('ue', 'cell')), may hold values from 0.2 to 5
- power_init: float32 [32, 4096], P(None, ('ue', 'cell')), may hold values from 0.01 to 2
- avg_init: float32 [65536], P(('ue', 'cell')), may hold values from 0.05 to 1
Outputs:
- avg_out: float32 [65536], P(('ue', 'cell'))
- power_out: float32 [32, 4096], P(None, ('ue', 'cell'))
Inputs may be any that keep to these rules, and one draw needn't show every extreme that they name: `near_blocks`: for each UE block, the entries in columns j * 4 to (j + 1) * 4 - 1 are distinct cell blocks, each equal to j modulo 4. `serve_block`: within the 2048 UEs of each aligned block, at most 192 have the same serving cell block, and some cell block serves exactly 192 of them.
All inputs are finite; a program needn't handle non-finite values.
Results may differ from a plain program's by a relative error of at most 0.002.
Values may be sent and summed in bfloat16 or wider, within the bound.
A program may use at most 128 MiB of HBM per device.

v0:
```python
import jax
import jax.numpy as jnp
from jax import lax
from jax.sharding import PartitionSpec as P

SLOTS = 4


NOISE_FLOOR = 0.5
KEEP_RATE = 0.7
NEW_RATE = 0.3


def send_records(levels, gain_box, average_box, cell_box):
    return (
        lax.all_to_all(levels, ("ue", "cell"), split_axis=1, concat_axis=1, tiled=True),
        lax.all_to_all(gain_box, ("ue", "cell"), split_axis=1, concat_axis=1, tiled=True),
        lax.all_to_all(average_box, ("ue", "cell"), split_axis=1, concat_axis=1, tiled=True),
        lax.all_to_all(cell_box, ("ue", "cell"), split_axis=1, concat_axis=1, tiled=True),
    )


def send_back(average_box):
    return lax.all_to_all(average_box, ("ue", "cell"), split_axis=1, concat_axis=1, tiled=True)


def interference(power_state, gains, near_local, ue_rows):
    ue_count = lax.axis_size("ue")
    subbands, width = power_state.shape
    low_power = power_state.astype(jnp.bfloat16)
    gathered = lax.all_gather(low_power, "ue", axis=1, tiled=True)
    power_table = gathered.reshape(subbands, ue_count, width).transpose(1, 0, 2)
    chosen = power_table[near_local]
    summed = lax.psum_scatter(
        lax.dot_general(
            chosen, gains, (((1, 3), (1, 2)), ((0,), (0,))), preferred_element_type=jnp.float32
        ).astype(jnp.bfloat16),
        "cell",
        scatter_dimension=0,
        tiled=True,
    ).astype(jnp.float32)
    return summed.transpose(1, 0, 2).reshape(subbands, ue_rows)


def attach(cells_flat, width):
    attach_map = (cells_flat[None, :] == jnp.arange(width, dtype=jnp.int32)[:, None]).astype(
        jnp.float32
    )
    unused = (cells_flat < 0).astype(jnp.float32)
    return (attach_map, unused)


def serve(levels_in, gain_row, average_row, attach_map, unused, power_state):
    subbands = power_state.shape[0]
    serving_power = jnp.dot(power_state, attach_map, precision=lax.Precision.HIGHEST)
    signal = gain_row[None, :] * serving_power
    log_rate = jnp.log1p(signal / (levels_in + NOISE_FLOOR))
    metric = log_rate / average_row[None, :]
    cell_load = jnp.dot(metric, attach_map.T, precision=lax.Precision.HIGHEST)
    spread_load = jnp.dot(cell_load, attach_map, precision=lax.Precision.HIGHEST) + unused[None, :]
    shares = metric / spread_load
    new_average = KEEP_RATE * average_row + NEW_RATE * jnp.sum(shares * log_rate, axis=0)
    demand = 1.0 + cell_load
    new_power = 0.5 * power_state + 0.5 * subbands * demand / jnp.sum(demand, axis=0, keepdims=True)
    return (new_average, new_power)


def on_device(gains, near_blocks, serve_block, serve_cell, serve_gain, power_init, avg_init):
    ue_count = lax.axis_size("ue")
    cell_count = lax.axis_size("cell")
    device_count = ue_count * cell_count
    ue_rows = serve_gain.shape[0]
    subbands, width = power_init.shape
    capacity = max(2, 3 * ue_rows // device_count)
    slot_total = device_count * capacity
    near_local = near_blocks // cell_count
    destination = serve_block[:, 0]
    matches = (destination[:, None] == jnp.arange(device_count, dtype=jnp.int32)[None, :]).astype(
        jnp.int32
    )
    position = jnp.sum(jnp.cumsum(matches, axis=0) * matches, axis=1) - 1
    slots = destination * capacity + position

    def pack(values, fill_value, dtype):
        filled = jnp.full((slot_total,), fill_value, dtype).at[slots].set(values)
        return filled.reshape(1, device_count, capacity)

    gain_box = pack(serve_gain, 0.0, jnp.float32)
    cell_box = pack(serve_cell, -1, jnp.int32)
    power_state = power_init
    average_home = avg_init
    for turn_index in range(SLOTS):
        levels = interference(power_state, gains, near_local, ue_rows)
        pack_filled = jnp.zeros((subbands, slot_total), jnp.float32).at[:, slots].set(levels)
        levels_in, gain_in, average_in, cells_in = send_records(
            pack_filled.reshape(subbands, device_count, capacity),
            gain_box,
            pack(average_home, 1.0, jnp.float32),
            cell_box,
        )
        attach_map, unused = attach(cells_in.reshape(slot_total), width)
        average_row, power_state = serve(
            levels_in.reshape(subbands, slot_total),
            gain_in.reshape(slot_total),
            average_in.reshape(slot_total),
            attach_map,
            unused,
            power_state,
        )
        returned = send_back(average_row.reshape(1, device_count, capacity))
        average_home = returned.reshape(slot_total)[slots]
    return (average_home, power_state)


def solution(mesh):
    return jax.shard_map(
        on_device,
        mesh=mesh,
        in_specs=(
            P("ue", "cell", None, None),
            P("ue", "cell"),
            P(("ue", "cell"), None),
            P(("ue", "cell")),
            P(("ue", "cell")),
            P(None, ("ue", "cell")),
            P(("ue", "cell")),
        ),
        out_specs=(P(("ue", "cell")), P(None, ("ue", "cell"))),
        check_vma=False,
    )
```

profile of v0, /device:TPU:0, one launch (start us, length us, event | category | flops | bytes accessed | tf_op | source)
XLA Modules:
  0.0 527.4 jit_solution(17181125096152518469)
XLA Ops:
  8.8 27.8 %all_gather.12 = bf16[32,1024]{1,0:T(8,128)(2,1)S(1)} all-gather(bf16[32,128]{1,0:T(8,128)(2,1)S(1)} %convert_element_type.48), channel_id=1, replica_groups=mesh['ue'=8,'cell'=4] {'ue'}, dimensions={1}, use_global_device_ids=true | all-gather | bytes 73728 | tf_op jit(solution)/shard_map/all_gather | solution.py:31
  37.6 5.5 %fusion.45 = bf16[64,32,128]{2,1,0:T(8,128)(2,1)} fusion(bf16[64,4,32,128]{3,2,1,0:T(8,128)(2,1)S(1)} %bitcast.141, bf16[64,4,128,128]{3,2,1,0:T(8,128)(2,1)} %param.7), kind=kOutput, calls=%fused_computation.76 | convolution fusion | flops 268697600 | bytes 11010048 | tf_op jit(solution)/shard_map/dot_general | solution.py:35
  43.2 9.1 %reduce-window.6 = s32[32,16,128]{2,1,0:T(8,128)S(1)} reduce-window(s32[32,16,128]{2,1,0:T(8,128)S(1)} %fusion.63, s32[]{:T(128)} %constant.16.clone.1), window={size=1x1x128 pad=0_0x0_0x127_0}, to_apply=%region_0.1 | reduce-window | flops 8323072 | bytes 524292 | tf_op jit(solution)/shard_map/reduce-window
  53.2 8.2 %scatter_custom_fusion.2 = s32[6144]{0:T(1024)S(1)} fusion(s32[2048]{0:T(1024)S(1)} %bitcast.153, s32[2048]{0:T(1024)} %param.10, s32[]{:T(128)} %constant.17.clone.1), kind=kCustom, calls=%fused_computation.133 | custom fusion | bytes 25088 | tf_op jit(solution)/shard_map/scatter | solution.py:85
  62.1 4.0 all-to-all-start.2
  66.1 8.2 %scatter_custom_fusion.1 = f32[6144]{0:T(1024)S(1)} fusion(s32[2048]{0:T(1024)S(1)} %bitcast.154, f32[2048]{0:T(1024)} %param.11, f32[]{:T(128)} %constant.20.clone.1), kind=kCustom, calls=%fused_computation.135 | custom fusion | bytes 25088 | tf_op jit(solution)/shard_map/scatter | solution.py:85
  75.1 5.8 %all-to-all-start.1 = ((f32[1,32,192]{2,0,1:T(1,128)}), f32[1,32,192]{2,0,1:T(1,128)S(1)}, u32[]{:S(2)}, u32[]{:S(2)}) async-start(f32[1,32,192]{2,0,1:T(1,128)} %reshape.197), calls=%async_computation.1 | async-start | bytes 65536 | tf_op jit(solution)/shard_map/all_to_all | solution.py:17
  80.9 8.2 %scatter_custom_fusion = f32[6144]{0:T(1024)S(1)} fusion(s32[2048]{0:T(1024)S(1)} %bitcast.155, f32[2048]{0:T(1024)} %param.13, f32[]{:T(128)} %constant.14.clone.1), kind=kCustom, calls=%fused_computation.143 | custom fusion | bytes 25088 | tf_op jit(solution)/shard_map/scatter | solution.py:85
  89.9 5.8 %all-to-all-start = ((f32[1,32,192]{2,0,1:T(1,128)}), f32[1,32,192]{2,0,1:T(1,128)S(1)}, u32[]{:S(2)}, u32[]{:S(2)}) async-start(f32[1,32,192]{2,0,1:T(1,128)} %reshape.196), calls=%async_computation | async-start | bytes 65536 | tf_op jit(solution)/shard_map/all_to_all | solution.py:18
  98.0 6.7 %scatter_custom_fusion.3 = f32[32,6144]{0,1:T(8,128)S(1)} fusion(s32[2048]{0:T(1024)S(1)} %bitcast.156, f32[2048,32]{1,0:T(8,128)} %copy.59, f32[]{:T(128)} %constant.20.clone.1), kind=kCustom, calls=%fused_computation.58 | custom fusion | bytes 786944 | tf_op jit(solution)/shard_map/scatter | solution.py:94
  104.7 2.2 copy.60
  106.9 5.8 %all-to-all-start.3 = ((f32[32,32,192]{2,0,1:T(8,128)}), f32[32,32,192]{2,0,1:T(8,128)S(1)}, u32[]{:S(2)}, u32[]{:S(2)}) async-start(f32[32,32,192]{2,0,1:T(8,128)} %copy.60), calls=%async_computation.4 | async-start | bytes 2097152 | tf_op jit(solution)/shard_map/all_to_all | solution.py:16
  113.8 25.2 %all-to-all-done.3 = f32[32,32,192]{2,0,1:T(8,128)S(1)} async-done(((f32[32,32,192]{2,0,1:T(8,128)}), f32[32,32,192]{2,0,1:T(8,128)S(1)}, u32[]{:S(2)}, u32[]{:S(2)}) %all-to-all-start.3) | async-done | bytes 786464 | tf_op jit(solution)/shard_map/all_to_all | solution.py:16
  141.5 1.8 add_reduce_fusion.3
  143.3 26.0 %all_gather.13 = bf16[32,1024]{1,0:T(8,128)(2,1)S(1)} all-gather(bf16[32,128]{1,0:T(8,128)(2,1)S(1)} %get-tuple-element.6), channel_id=1, replica_groups=mesh['ue'=8,'cell'=4] {'ue'}, dimensions={1}, use_global_device_ids=true | all-gather | bytes 73728 | tf_op jit(solution)/shard_map/all_gather | solution.py:31
  170.3 5.5 %fusion.46 = bf16[64,32,128]{2,1,0:T(8,128)(2,1)} fusion(bf16[64,4,32,128]{3,2,1,0:T(8,128)(2,1)S(1)} %bitcast.142, bf16[64,4,128,128]{3,2,1,0:T(8,128)(2,1)} %param.7), kind=kOutput, calls=%fused_computation.77 | convolution fusion | flops 268697600 | bytes 11010048 | tf_op jit(solution)/shard_map/dot_general | solution.py:35
  177.9 2.5 all-to-all-start.4
  180.4 7.2 %all-to-all-done.4 = f32[1,32,192]{2,0,1:T(1,128)S(1)} async-done(((f32[1,32,192]{2,0,1:T(1,128)}), f32[1,32,192]{2,0,1:T(1,128)S(1)}, u32[]{:S(2)}, u32[]{:S(2)}) %all-to-all-start.4) | async-done | bytes 24608 | tf_op jit(solution)/shard_map/all_to_all | solution.py:24
  187.8 11.8 %gather_fusion.1 = f32[2048]{0:T(1024)S(1)} fusion(f32[6144]{0:T(1024)S(1)} %reshape.203, s32[2048]{0:T(1024)S(1)} %broadcast_clamp_fusion), kind=kCustom, calls=%fused_computation.1 | custom fusion | bytes 24576 | tf_op jit(solution)/shard_map/gather | solution.py:111
  199.6 8.1 %scatter_custom_fusion.4 = f32[6144]{0:T(1024)S(1)} fusion(s32[2048]{0:T(1024)S(1)} %bitcast.158, f32[2048]{0:T(1024)S(1)} %gather_fusion.1, f32[]{:T(128)} %constant.14.clone.1), kind=kCustom, calls=%fused_computation.141 | custom fusion | bytes 24580 | tf_op jit(solution)/shard_map/scatter | solution.py:85
  208.4 2.6 all-to-all-start.5
  213.2 6.7 %scatter_custom_fusion.5 = f32[32,6144]{0,1:T(8,128)S(1)} fusion(s32[2048]{0:T(1024)S(1)} %bitcast.159, f32[2048,32]{1,0:T(8,128)} %copy.64, f32[]{:T(128)} %constant.20.clone.1), kind=kCustom, calls=%fused_computation.56 | custom fusion | bytes 786944 | tf_op jit(solution)/shard_map/scatter | solution.py:94
  219.9 2.2 copy.65
  222.1 5.8 %all-to-all-start.6 = ((f32[32,32,192]{2,0,1:T(8,128)}), f32[32,32,192]{2,0,1:T(8,128)S(1)}, u32[]{:S(2)}, u32[]{:S(2)}) async-start(f32[32,32,192]{2,0,1:T(8,128)} %copy.65), calls=%async_computation.8 | async-start | bytes 2097152 | tf_op jit(solution)/shard_map/all_to_all | solution.py:16
  228.4 25.8 %all-to-all-done.6 = f32[32,32,192]{2,0,1:T(8,128)S(1)} async-done(((f32[32,32,192]{2,0,1:T(8,128)}), f32[32,32,192]{2,0,1:T(8,128)S(1)}, u32[]{:S(2)}, u32[]{:S(2)}) %all-to-all-start.6) | async-done | bytes 786464 | tf_op jit(solution)/shard_map/all_to_all | solution.py:16
  258.5 26.0 %all_gather.14 = bf16[32,1024]{1,0:T(8,128)(2,1)S(1)} all-gather(bf16[32,128]{1,0:T(8,128)(2,1)S(1)} %get-tuple-element.4), channel_id=1, replica_groups=mesh['ue'=8,'cell'=4] {'ue'}, dimensions={1}, use_global_device_ids=true | all-gather | bytes 73728 | tf_op jit(solution)/shard_map/all_gather | solution.py:31
  285.5 5.5 %fusion.47 = bf16[64,32,128]{2,1,0:T(8,128)(2,1)} fusion(bf16[64,4,32,128]{3,2,1,0:T(8,128)(2,1)S(1)} %bitcast.143, bf16[64,4,128,128]{3,2,1,0:T(8,128)(2,1)} %param.7), kind=kOutput, calls=%fused_computation.78 | convolution fusion | flops 268697600 | bytes 11010048 | tf_op jit(solution)/shard_map/dot_general | solution.py:35
  292.5 9.2 %all_to_all.76 = f32[1,32,192]{2,0,1:T(1,128)S(1)} all-to-all(f32[1,32,192]{2,0,1:T(1,128)S(1)} %multiply_add_fusion.2), channel_id=1, replica_groups=mesh['ue'=8,'cell'=4] {'ue','cell'}, dimensions={1} | all-to-all | bytes 49152 | tf_op jit(solution)/shard_map/all_to_all | solution.py:24
  301.8 11.8 %gather_fusion.3 = f32[2048]{0:T(1024)S(1)} fusion(f32[6144]{0:T(1024)S(1)} %reshape.209, s32[2048]{0:T(1024)S(1)} %broadcast_clamp_fusion), kind=kCustom, calls=%fused_computation.3 | custom fusion | bytes 24576 | tf_op jit(solution)/shard_map/gather | solution.py:111
  313.6 8.1 %scatter_custom_fusion.6 = f32[6144]{0:T(1024)S(1)} fusion(s32[2048]{0:T(1024)S(1)} %bitcast.160, f32[2048]{0:T(1024)S(1)} %gather_fusion.3, f32[]{:T(128)} %constant.14.clone.1), kind=kCustom, calls=%fused_computation.139 | custom fusion | bytes 24580 | tf_op jit(solution)/shard_map/scatter | solution.py:85
  322.4 2.6 all-to-all-start.8
  327.3 6.7 %scatter_custom_fusion.7 = f32[32,6144]{0,1:T(8,128)S(1)} fusion(s32[2048]{0:T(1024)S(1)} %bitcast.161, f32[2048,32]{1,0:T(8,128)} %copy.69, f32[]{:T(128)} %constant.20.clone.1), kind=kCustom, calls=%fused_computation.54 | custom fusion | bytes 786944 | tf_op jit(solution)/shard_map/scatter | solution.py:94
  334.0 2.2 copy.70
  336.2 5.8 %all-to-all-start.9 = ((f32[32,32,192]{2,0,1:T(8,128)}), f32[32,32,192]{2,0,1:T(8,128)S(1)}, u32[]{:S(2)}, u32[]{:S(2)}) async-start(f32[32,32,192]{2,0,1:T(8,128)} %copy.70), calls=%async_computation.12 | async-start | bytes 2097152 | tf_op jit(solution)/shard_map/all_to_all | solution.py:16
  342.5 25.8 %all-to-all-done.9 = f32[32,32,192]{2,0,1:T(8,128)S(1)} async-done(((f32[32,32,192]{2,0,1:T(8,128)}), f32[32,32,192]{2,0,1:T(8,128)S(1)}, u32[]{:S(2)}, u32[]{:S(2)}) %all-to-all-start.9) | async-done | bytes 786464 | tf_op jit(solution)/shard_map/all_to_all | solution.py:16
  372.6 26.0 %all_gather.15 = bf16[32,1024]{1,0:T(8,128)(2,1)S(1)} all-gather(bf16[32,128]{1,0:T(8,128)(2,1)S(1)} %get-tuple-element.2), channel_id=1, replica_groups=mesh['ue'=8,'cell'=4] {'ue'}, dimensions={1}, use_global_device_ids=true | all-gather | bytes 73728 | tf_op jit(solution)/shard_map/all_gather | solution.py:31
  399.6 5.5 %fusion.48 = bf16[64,32,128]{2,1,0:T(8,128)(2,1)} fusion(bf16[64,4,32,128]{3,2,1,0:T(8,128)(2,1)S(1)} %bitcast.140, bf16[64,4,128,128]{3,2,1,0:T(8,128)(2,1)} %param.7), kind=kOutput, calls=%fused_computation.79 | convolution fusion | flops 268697600 | bytes 11010048 | tf_op jit(solution)/shard_map/dot_general | solution.py:35
  406.6 9.2 %all_to_all.77 = f32[1,32,192]{2,0,1:T(1,128)S(1)} all-to-all(f32[1,32,192]{2,0,1:T(1,128)S(1)} %multiply_add_fusion.1), channel_id=1, replica_groups=mesh['ue'=8,'cell'=4] {'ue','cell'}, dimensions={1} | all-to-all | bytes 49152 | tf_op jit(solution)/shard_map/all_to_all | solution.py:24
  415.9 11.8 %gather_fusion.5 = f32[2048]{0:T(1024)S(1)} fusion(f32[6144]{0:T(1024)S(1)} %reshape.215, s32[2048]{0:T(1024)S(1)} %broadcast_clamp_fusion), kind=kCustom, calls=%fused_computation.5 | custom fusion | bytes 24576 | tf_op jit(solution)/shard_map/gather | solution.py:111
  427.7 8.1 %scatter_custom_fusion.8 = f32[6144]{0:T(1024)S(1)} fusion(s32[2048]{0:T(1024)S(1)} %bitcast.162, f32[2048]{0:T(1024)S(1)} %gather_fusion.5, f32[]{:T(128)} %constant.14.clone.1), kind=kCustom, calls=%fused_computation.137 | custom fusion | bytes 24580 | tf_op jit(solution)/shard_map/scatter | solution.py:85
  436.5 2.6 all-to-all-start.11
  441.3 6.7 %scatter_custom_fusion.9 = f32[32,6144]{0,1:T(8,128)S(1)} fusion(s32[2048]{0:T(1024)S(1)} %bitcast.163, f32[2048,32]{1,0:T(8,128)} %copy.74, f32[]{:T(128)} %constant.20.clone.1), kind=kCustom, calls=%fused_computation.52 | custom fusion | bytes 786944 | tf_op jit(solution)/shard_map/scatter | solution.py:94
  448.0 2.2 copy.75
  450.3 6.1 %all-to-all-start.12 = ((f32[32,32,192]{2,0,1:T(8,128)}), f32[32,32,192]{2,0,1:T(8,128)S(1)}, u32[]{:S(2)}, u32[]{:S(2)}) async-start(f32[32,32,192]{2,0,1:T(8,128)} %copy.75), calls=%async_computation.16 | async-start | bytes 2097152 | tf_op jit(solution)/shard_map/all_to_all | solution.py:16
  456.5 26.1 %all-to-all-done.12 = f32[32,32,192]{2,0,1:T(8,128)S(1)} async-done(((f32[32,32,192]{2,0,1:T(8,128)}), f32[32,32,192]{2,0,1:T(8,128)S(1)}, u32[]{:S(2)}, u32[]{:S(2)}) %all-to-all-start.12) | async-done | bytes 786464 | tf_op jit(solution)/shard_map/all_to_all | solution.py:16
  488.9 3.6 all-to-all-start.13
  493.1 6.6 %all-to-all-done.13 = f32[1,32,192]{2,0,1:T(1,128)S(1)} async-done(((f32[1,32,192]{2,0,1:T(1,128)}), f32[1,32,192]{2,0,1:T(1,128)S(1)}, u32[]{:S(2)}, u32[]{:S(2)}) %all-to-all-start.13) | async-done | bytes 24608 | tf_op jit(solution)/shard_map/all_to_all | solution.py:24
  499.9 20.5 %gather_fusion.7 = f32[2048]{0:T(1024)} fusion(f32[6144]{0:T(1024)S(1)} %reshape.221, s32[2048]{0:T(1024)S(1)} %broadcast_clamp_fusion), kind=kCustom, calls=%fused_computation.7 | custom fusion | bytes 24576 | tf_op jit(solution)/shard_map/gather | solution.py:111
  (118 shorter events, 45.1 us)
Async XLA Ops:
  7.2 88.6 %reduce-scatter.5.cloned.1.call-start = ((), (), s32[]{:S(2)}) async-start(), calls=%async_computation.18 | async-start | bytes 655360 | tf_op jit(solution)/shard_map/reduce_scatter | solution.py:34
  37.6 5.6 %copy-start = (s32[2048,1]{0,1:T(1,128)S(1)}, s32[2048,1]{0,1:T(1,128)}, u32[]{:S(2)}) copy-start(s32[2048,1]{0,1:T(1,128)} %param.9) | copy-start | bytes 24580
  62.1 12.9 %all-to-all-start.2 = ((s32[1,32,192]{2,0,1:T(1,128)}), s32[1,32,192]{2,0,1:T(1,128)S(1)}, u32[]{:S(2)}, u32[]{:S(2)}) async-start(s32[1,32,192]{2,0,1:T(1,128)} %reshape.198), calls=%async_computation.2 | async-start | bytes 65536 | tf_op jit(solution)/shard_map/all_to_all | solution.py:19
  75.1 14.8 %all-to-all-start.1 = ((f32[1,32,192]{2,0,1:T(1,128)}), f32[1,32,192]{2,0,1:T(1,128)S(1)}, u32[]{:S(2)}, u32[]{:S(2)}) async-start(f32[1,32,192]{2,0,1:T(1,128)} %reshape.197), calls=%async_computation.1 | async-start | bytes 65536 | tf_op jit(solution)/shard_map/all_to_all | solution.py:17
  89.9 17.1 %all-to-all-start = ((f32[1,32,192]{2,0,1:T(1,128)}), f32[1,32,192]{2,0,1:T(1,128)S(1)}, u32[]{:S(2)}, u32[]{:S(2)}) async-start(f32[1,32,192]{2,0,1:T(1,128)} %reshape.196), calls=%async_computation | async-start | bytes 65536 | tf_op jit(solution)/shard_map/all_to_all | solution.py:18
  106.9 32.1 %all-to-all-start.3 = ((f32[32,32,192]{2,0,1:T(8,128)}), f32[32,32,192]{2,0,1:T(8,128)S(1)}, u32[]{:S(2)}, u32[]{:S(2)}) async-start(f32[32,32,192]{2,0,1:T(8,128)} %copy.60), calls=%async_computation.4 | async-start | bytes 2097152 | tf_op jit(solution)/shard_map/all_to_all | solution.py:16
  112.8 98.2 %reduce-scatter.7.cloned.1.call-start = ((), (), s32[]{:S(2)}) async-start(), calls=%async_computation.19 | async-start | bytes 655360 | tf_op jit(solution)/shard_map/reduce_scatter | solution.py:34
  113.5 26.7 %copy-start.1 = (f32[32,128]{1,0:T(8,128)S(1)}, f32[32,128]{1,0:T(8,128)}, u32[]{:S(2)}) copy-start(f32[32,128]{1,0:T(8,128)} %param.12) | copy-start | bytes 49156
  177.9 9.7 %all-to-all-start.4 = ((f32[1,32,192]{2,0,1:T(1,128)}), f32[1,32,192]{2,0,1:T(1,128)S(1)}, u32[]{:S(2)}, u32[]{:S(2)}) async-start(f32[1,32,192]{2,0,1:T(1,128)} %multiply_add_fusion.3), calls=%async_computation.5 | async-start | bytes 65536 | tf_op jit(solution)/shard_map/all_to_all | solution.py:24
  208.4 13.8 %all-to-all-start.5 = ((f32[1,32,192]{2,0,1:T(1,128)}), f32[1,32,192]{2,0,1:T(1,128)S(1)}, u32[]{:S(2)}, u32[]{:S(2)}) async-start(f32[1,32,192]{2,0,1:T(1,128)} %reshape.204), calls=%async_computation.6 | async-start | bytes 65536 | tf_op jit(solution)/shard_map/all_to_all | solution.py:18
  222.1 32.1 %all-to-all-start.6 = ((f32[32,32,192]{2,0,1:T(8,128)}), f32[32,32,192]{2,0,1:T(8,128)S(1)}, u32[]{:S(2)}, u32[]{:S(2)}) async-start(f32[32,32,192]{2,0,1:T(8,128)} %copy.65), calls=%async_computation.8 | async-start | bytes 2097152 | tf_op jit(solution)/shard_map/all_to_all | solution.py:16
  228.0 97.0 %reduce-scatter.9.cloned.1.call-start = ((), (), s32[]{:S(2)}) async-start(), calls=%async_computation.20 | async-start | bytes 655360 | tf_op jit(solution)/shard_map/reduce_scatter | solution.py:34
  322.4 13.8 %all-to-all-start.8 = ((f32[1,32,192]{2,0,1:T(1,128)}), f32[1,32,192]{2,0,1:T(1,128)S(1)}, u32[]{:S(2)}, u32[]{:S(2)}) async-start(f32[1,32,192]{2,0,1:T(1,128)} %reshape.210), calls=%async_computation.10 | async-start | bytes 65536 | tf_op jit(solution)/shard_map/all_to_all | solution.py:18
  336.2 32.1 %all-to-all-start.9 = ((f32[32,32,192]{2,0,1:T(8,128)}), f32[32,32,192]{2,0,1:T(8,128)S(1)}, u32[]{:S(2)}, u32[]{:S(2)}) async-start(f32[32,32,192]{2,0,1:T(8,128)} %copy.70), calls=%async_computation.12 | async-start | bytes 2097152 | tf_op jit(solution)/shard_map/all_to_all | solution.py:16
  342.0 97.0 %reduce-scatter.11.cloned.1.call-start = ((), (), s32[]{:S(2)}) async-start(), calls=%async_computation.21 | async-start | bytes 655360 | tf_op jit(solution)/shard_map/reduce_scatter | solution.py:34
  436.5 13.8 %all-to-all-start.11 = ((f32[1,32,192]{2,0,1:T(1,128)}), f32[1,32,192]{2,0,1:T(1,128)S(1)}, u32[]{:S(2)}, u32[]{:S(2)}) async-start(f32[1,32,192]{2,0,1:T(1,128)} %reshape.216), calls=%async_computation.14 | async-start | bytes 65536 | tf_op jit(solution)/shard_map/all_to_all | solution.py:18
  450.3 32.3 %all-to-all-start.12 = ((f32[32,32,192]{2,0,1:T(8,128)}), f32[32,32,192]{2,0,1:T(8,128)S(1)}, u32[]{:S(2)}, u32[]{:S(2)}) async-start(f32[32,32,192]{2,0,1:T(8,128)} %copy.75), calls=%async_computation.16 | async-start | bytes 2097152 | tf_op jit(solution)/shard_map/all_to_all | solution.py:16
  488.9 10.9 %all-to-all-start.13 = ((f32[1,32,192]{2,0,1:T(1,128)}), f32[1,32,192]{2,0,1:T(1,128)S(1)}, u32[]{:S(2)}, u32[]{:S(2)}) async-start(f32[1,32,192]{2,0,1:T(1,128)} %multiply_add_fusion), calls=%async_computation.17 | async-start | bytes 65536 | tf_op jit(solution)/shard_map/all_to_all | solution.py:24
Sparse Core Ops, SparseCore 0:
  43.3 21.0 reduce-scatter.4
  176.0 19.1 reduce-scatter.6
  291.2 19.1 reduce-scatter.8
  405.3 19.1 reduce-scatter.10
where the time goes:
time: 535 us; the launch traced here: 527 us
  local copies, waits for them, and re-layouts  160 us (30%)
  blocking collectives  124 us (23%)
  waiting for transfers between devices  117 us (22%)
  starting transfers between devices  54.1 us (10%)
  matrix products  39.8 us (7%)
  other arithmetic  17.9 us (3%)
  between operations  14.9 us (3%)
    all_gather x4, blocking collectives, interference(): gathered = lax.all_gather(low_power, 'ue', axis=1, tiled=True)  106 us
    all_to_all x4, waiting for transfers between devices, send_records(): lax.all_to_all(levels, ('ue', 'cell'), split_axis=1, concat_axis=1, tiled...  103 us
    gather x4, local copies, waits for them, and re-layouts, on_device(): average_home = returned.reshape(slot_total)[slots]  55.9 us
    scatter x6, local copies, waits for them, and re-layouts, pack(): filled = jnp.full((slot_total,), fill_value, dtype).at[slots].set(values)  49 us
    scatter x4, local copies, waits for them, and re-layouts, on_device(): jnp.zeros((subbands, slot_total), jnp.float32).at[:, slots].set(levels)  26.9 us
    all_to_all x4, starting transfers between devices, send_records(): lax.all_to_all(levels, ('ue', 'cell'), split_axis=1, concat_axis=1, tiled...  23.6 us
    dot_general x4, matrix products, interference(): lax.dot_general(chosen, gains, (((1, 3), (1, 2)), ((0,), (0,))), preferre...  22.2 us
    all_to_all x2, blocking collectives, send_back(): lax.all_to_all(average_box, ('ue', 'cell'), split_axis=1, concat_axis=1,...  18.3 us
  transfers between devices with their start and end apart: 16, of which 6 were waited for; matrix products, arithmetic and copies ran while one was open for 28% of the time, Pallas kernels for 0%

commit v1 on v0

v1 whole, which is shorter than its diff:
```python
import functools

import jax
import jax.numpy as jnp
from jax import lax
from jax.experimental import pallas as pl
from jax.experimental.pallas import tpu as pltpu
from jax.sharding import PartitionSpec as P

SLOTS = 4
NOISE_FLOOR = 0.5
KEEP_RATE = 0.7
NEW_RATE = 0.3
MESH = pl.DeviceIdType.MESH


def planner(
    ue_count, cell_count,
    gains_hbm, near, block_ref, cell_ref, gain_ref, power_ref, avg_ref,
    avg_out, power_out,
    gains, high, low, power, loads, tails, mine, parts_in, parts_out, terms_in, terms_out,
    levels, signal_power, log_rates, metrics, spread, pick_cell, put_cell,
    gains_sem, terms_send, terms_recv, parts_send, parts_recv, loads_send, loads_recv,
    tails_send, tails_recv,
):
    device_count = ue_count * cell_count
    ue_at, cell_at = lax.axis_index("ue"), lax.axis_index("cell")
    me = ue_at * cell_count + cell_at
    home_blocks, subbands, width = levels.shape
    near_count = near.shape[0] // gains.shape[0]
    pairs = home_blocks // 2
    f32, bf16 = jnp.float32, jnp.bfloat16

    def device(number):
        return (number // cell_count, lax.rem(number, cell_count))

    barrier = pltpu.get_barrier_semaphore()

    def greet(step, carry):
        pl.semaphore_signal(
            barrier, inc=1, device_id=device(lax.rem(me + step, device_count)), device_id_type=MESH
        )
        return carry

    lax.fori_loop(1, device_count, greet, 0)

    def gains_copy(chunk):
        rows = pl.ds(chunk * home_blocks, home_blocks)
        return pltpu.make_async_copy(gains_hbm.at[rows], gains.at[rows], gains_sem.at[chunk])

    for step in range(1, cell_count + 1):
        gains_copy(lax.rem(cell_at + step, cell_count)).start()
    pl.semaphore_wait(barrier, device_count - 1)

    def spread_copy(table, send_sem, recv_sem, step):
        return pltpu.make_async_remote_copy(
            src_ref=table.at[me], dst_ref=table.at[me],
            send_sem=send_sem.at[step], recv_sem=recv_sem.at[step],
            device_id=device(lax.rem(me + step, device_count)), device_id_type=MESH,
        )

    def spread_arrival(table, send_sem, recv_sem, step):
        source = lax.rem(me - step + device_count, device_count)
        return pltpu.make_async_remote_copy(
            src_ref=table.at[source], dst_ref=table.at[source],
            send_sem=send_sem.at[step], recv_sem=recv_sem.at[step],
            device_id=device(source), device_id_type=MESH,
        )

    main = (loads, loads_send, loads_recv)
    rest = (tails, tails_send, tails_recv)

    def split_load(value):
        top = value.astype(bf16)
        loads[me] = top
        tails[me] = (value - top.astype(f32)).astype(bf16)

    def whole_load(block):
        return loads[block].astype(f32) + tails[block].astype(f32)

    def parts_copy(owner):
        step = lax.rem(owner - me + device_count, device_count)
        return pltpu.make_async_remote_copy(
            src_ref=parts_out.at[owner], dst_ref=parts_in.at[step],
            send_sem=parts_send.at[step], recv_sem=parts_recv.at[step],
            device_id=device(owner), device_id_type=MESH,
        )

    def terms_copy(step):
        target = lax.rem(cell_at + step, cell_count)
        return pltpu.make_async_remote_copy(
            src_ref=terms_out.at[step], dst_ref=terms_in.at[step],
            send_sem=terms_send.at[step], recv_sem=terms_recv.at[step],
            device_id=(ue_at, target), device_id_type=MESH,
        )

    def each_peer(action):
        def body(step, carry):
            action(step)
            return carry

        lax.fori_loop(1, device_count, body, 0)

    def set_power(block, value):
        power[block] = value
        top = value.astype(bf16)
        high[block] = top
        low[block] = (value - top.astype(f32)).astype(bf16)

    def next_power(value, load):
        demand = 1.0 + load
        scale = (0.5 * subbands) / jnp.sum(demand, axis=0, keepdims=True)
        return 0.5 * value + demand * scale

    mine[...] = power_ref[...]
    split_load(power_ref[...])
    each_peer(lambda step: spread_copy(*main, step).start())
    each_peer(lambda step: spread_copy(*rest, step).start())
    spots = lax.broadcasted_iota(jnp.int32, (width, width), 0)
    for home in range(home_blocks):
        hot = (spots == cell_ref[home]).astype(f32)
        columns = slice((home % 2) * width, (home % 2 + 1) * width)
        pick_cell[home // 2, 0:width, columns] = hot.astype(bf16)
        pick_cell[home // 2, width : 2 * width, columns] = hot.astype(bf16)
        put_cell[home * width : (home + 1) * width, :] = hot.T.astype(bf16)
        avg_out[home] = avg_ref[home]
    each_peer(lambda step: spread_arrival(*main, step).wait_recv())

    def start_high(block, carry):
        high[block] = loads[block]
        return carry

    lax.fori_loop(0, device_count, start_high, 0)
    each_peer(lambda step: spread_copy(*main, step).wait_send())

    def finish_power(turn):
        each_peer(lambda step: spread_arrival(*rest, step).wait_recv())

        @pl.when(turn == 0)
        def _():
            def first(block, carry):
                set_power(block, whole_load(block))
                return carry

            lax.fori_loop(0, device_count, first, 0)

        @pl.when(turn > 0)
        def _():
            def later(block, carry):
                set_power(block, next_power(power[block], whole_load(block)))
                return carry

            lax.fori_loop(0, device_count, later, 0)

        set_power(me, mine[...])
        each_peer(lambda step: spread_copy(*rest, step).wait_send())

    def terms(target, step):
        def body(group, carry):
            for inner in range(4):
                home = group * 4 + inner
                block = target * home_blocks + home
                chosen = jnp.concatenate(
                    [high[near[block * near_count + k]] for k in range(near_count)], axis=1
                )
                total = jnp.dot(chosen, gains[block], preferred_element_type=f32)
                if step == cell_count:
                    levels[home] = total
                else:
                    terms_out[step, home] = total.astype(bf16)
            return carry

        lax.fori_loop(0, home_blocks // 4, body, 0)

    group_blocks = 16

    def gather(table, result):
        def body(pair, carry):
            names = jnp.concatenate([block_ref[2 * pair], block_ref[2 * pair + 1]], axis=1)
            total = jnp.zeros((subbands, 2 * width), f32)
            for first in range(0, device_count, group_blocks):
                left = table(first)
                found = jnp.dot(
                    left, pick_cell[pair, 0 : left.shape[1], :], preferred_element_type=f32
                )
                for inner in range(group_blocks):
                    total = jnp.where(
                        names == first + inner,
                        found[inner * subbands : (inner + 1) * subbands],
                        total,
                    )
            result[2 * pair] = total[:, :width]
            result[2 * pair + 1] = total[:, width:]
            return carry

        lax.fori_loop(0, pairs, body, 0)

    def power_rows(first):
        rows = slice(first, first + group_blocks)
        both = jnp.concatenate([high[rows], low[rows]], axis=2)
        return both.reshape(group_blocks * subbands, 2 * width)

    def load_rows(first):
        return loads[first : first + group_blocks].reshape(group_blocks * subbands, width)

    def finish_average():
        gather(load_rows, spread)
        for home in range(home_blocks):
            share = metrics[home] / spread[home]
            gained = jnp.sum(share * log_rates[home], axis=0, keepdims=True)
            avg_out[home] = KEEP_RATE * avg_out[home] + NEW_RATE * gained

    piece = 8

    def slot(turn, carry):
        for step in range(1, cell_count + 1):
            target = lax.rem(cell_at + step, cell_count)

            @pl.when(turn == 0)
            def _():
                gains_copy(target).wait()

            terms(target, step)
            if step < cell_count:
                terms_copy(step).start()

        @pl.when(turn > 0)
        def _():
            finish_average()

        finish_power(turn)
        gather(power_rows, signal_power)
        for step in range(1, cell_count):
            terms_copy(step).wait_recv()
        for home in range(home_blocks):
            level = levels[home]
            for step in range(1, cell_count):
                level = level + terms_in[step, home].astype(f32)
            signal = gain_ref[home] * signal_power[home]
            rate = jnp.log1p(signal / (level + NOISE_FLOOR))
            log_rates[home] = rate
            metrics[home] = rate / avg_out[home]
        names = jnp.concatenate([block_ref[home] for home in range(home_blocks)], axis=1)

        def scatter(index, inner_carry):
            first = lax.rem(me // piece + 1 + index, device_count // piece) * piece
            metric = jnp.concatenate([metrics[home] for home in range(home_blocks)], axis=1)
            left = jnp.concatenate(
                [
                    jnp.where(names == first + inner, metric, 0.0).astype(bf16)
                    for inner in range(piece)
                ],
                axis=0,
            )
            summed = jnp.dot(left, put_cell[...], preferred_element_type=f32)
            for inner in range(piece):
                owner = first + inner
                parts_out[owner] = summed[inner * subbands : (inner + 1) * subbands].astype(bf16)

                @pl.when(owner != me)
                def _():
                    parts_copy(owner).start()

            return inner_carry

        lax.fori_loop(0, device_count // piece, scatter, 0)
        for step in range(1, cell_count):
            terms_copy(step).wait_send()

        def add(step, total):
            parts_copy(lax.rem(me + step, device_count)).wait_recv()
            return total + parts_in[step].astype(f32)

        load = lax.fori_loop(1, device_count, add, parts_out[me].astype(f32))
        split_load(load)
        each_peer(lambda step: spread_copy(*main, step).start())

        @pl.when(turn < SLOTS - 1)
        def _():
            each_peer(lambda step: spread_copy(*rest, step).start())

        mine[...] = next_power(mine[...], load)
        each_peer(lambda step: parts_copy(lax.rem(me + step, device_count)).wait_send())
        each_peer(lambda step: spread_arrival(*main, step).wait_recv())

        @pl.when(turn < SLOTS - 1)
        def _():
            def update(block, inner_carry):
                high[block] = next_power(power[block], loads[block].astype(f32)).astype(bf16)
                return inner_carry

            lax.fori_loop(0, device_count, update, 0)
            high[me] = mine[...].astype(bf16)

        each_peer(lambda step: spread_copy(*main, step).wait_send())
        return carry

    lax.fori_loop(0, SLOTS, slot, 0)
    finish_average()
    power_out[...] = mine[...]


def on_device(gains, near_blocks, serve_block, serve_cell, serve_gain, power_init, avg_init):
    ue_count = lax.axis_size("ue")
    cell_count = lax.axis_size("cell")
    device_count = ue_count * cell_count
    blocks, near_count, width, _ = gains.shape
    rows = serve_gain.shape[0]
    homes = rows // width
    subbands = power_init.shape[0]
    f32, bf16 = jnp.float32, jnp.bfloat16
    in_vmem = pl.BlockSpec(memory_space=pltpu.VMEM)
    table = (device_count, subbands, width)
    home = (homes, subbands, width)
    row = (homes, 1, width)
    average, power = pl.pallas_call(
        functools.partial(planner, ue_count, cell_count),
        out_shape=(
            jax.ShapeDtypeStruct(row, f32),
            jax.ShapeDtypeStruct(power_init.shape, f32),
        ),
        in_specs=[
            pl.BlockSpec(memory_space=pl.ANY),
            pl.BlockSpec(memory_space=pltpu.SMEM),
        ]
        + [in_vmem] * 5,
        out_specs=(in_vmem, in_vmem),
        scratch_shapes=[
            pltpu.VMEM((blocks, near_count * width, width), bf16),
            pltpu.VMEM(table, bf16),
            pltpu.VMEM(table, bf16),
            pltpu.VMEM(table, f32),
            pltpu.VMEM(table, bf16),
            pltpu.VMEM(table, bf16),
            pltpu.VMEM((subbands, width), f32),
            pltpu.VMEM(table, bf16),
            pltpu.VMEM(table, bf16),
            pltpu.VMEM((cell_count,) + home, bf16),
            pltpu.VMEM((cell_count,) + home, bf16),
            pltpu.VMEM(home, f32),
            pltpu.VMEM(home, f32),
            pltpu.VMEM(home, f32),
            pltpu.VMEM(home, f32),
            pltpu.VMEM(home, f32),
            pltpu.VMEM((homes // 2, 2 * width, 2 * width), bf16),
            pltpu.VMEM((rows, width), bf16),
            pltpu.SemaphoreType.DMA((cell_count,)),
            pltpu.SemaphoreType.DMA((cell_count,)),
            pltpu.SemaphoreType.DMA((cell_count,)),
            pltpu.SemaphoreType.DMA((device_count,)),
            pltpu.SemaphoreType.DMA((device_count,)),
            pltpu.SemaphoreType.DMA((device_count,)),
            pltpu.SemaphoreType.DMA((device_count,)),
            pltpu.SemaphoreType.DMA((device_count,)),
            pltpu.SemaphoreType.DMA((device_count,)),
        ],
        compiler_params=pltpu.CompilerParams(
            collective_id=0, has_side_effects=True, vmem_limit_bytes=48 * 1024 * 1024
        ),
    )(
        gains.reshape(blocks, near_count * width, width),
        near_blocks.reshape(-1),
        serve_block.reshape(row),
        serve_cell.reshape(row),
        serve_gain.reshape(row),
        power_init,
        avg_init.reshape(row),
    )
    return (average.reshape(rows), power)


def solution(mesh):
    return jax.shard_map(
        on_device,
        mesh=mesh,
        in_specs=(
            P("ue", "cell", None, None),
            P("ue", "cell"),
            P(("ue", "cell"), None),
            P(("ue", "cell")),
            P(("ue", "cell")),
            P(None, ("ue", "cell")),
            P(("ue", "cell")),
        ),
        out_specs=(P(("ue", "cell")), P(None, ("ue", "cell"))),
        check_vma=False,
    )
```

time: 535 us -> 138 us (0.26); the launches traced: 527 us -> 138 us
  local copies, waits for them, and re-layouts: 160 us -> 5.58 us
  Pallas kernels: 0 us -> 131 us
  blocking collectives: 124 us -> 0 us
  waiting for transfers between devices: 117 us -> 0 us
  starting transfers between devices: 54.1 us -> 0 us
  matrix products: 39.8 us -> 0 us
  other arithmetic: 17.9 us -> 0 us
  between operations: 14.9 us -> 0.65 us
    pallas_call x0 -> x1, Pallas kernels: none -> 131 us  [on_device(): pl.pallas_call(functools.partial(planner, ue_count, cell_count), out_shap...]
    all_to_all x12 -> x0, waiting for transfers between devices: 117 us -> none  [the longest x4 103 us: send_records(): lax.all_to_all(levels, ('ue', 'cell'), split_axis=1, concat_axis=1, tiled...]
    all_gather x4 -> x0, blocking collectives: 106 us -> none  [interference(): gathered = lax.all_gather(low_power, 'ue', axis=1, tiled=True)]
    scatter x10 -> x0, local copies, waits for them, and re-layouts: 75.9 us -> none  [the longest x6 49 us: pack(): filled = jnp.full((slot_total,), fill_value, dtype).at[slots].set(values)]
    gather x8 -> x0, local copies, waits for them, and re-layouts: 59.8 us -> none  [the longest x4 55.9 us: on_device(): average_home = returned.reshape(slot_total)[slots]]
    all_to_all x12 -> x0, starting transfers between devices: 53.1 us -> none  [the longest x4 23.6 us: send_records(): lax.all_to_all(levels, ('ue', 'cell'), split_axis=1, concat_axis=1, tiled...]
    dot_general x16 -> x0, matrix products: 39.8 us -> none  [the longest x4 22.2 us: interference(): lax.dot_general(chosen, gains, (((1, 3), (1, 2)), ((0,), (0,))), preferre...]
    reshape x18 -> x1, local copies, waits for them, and re-layouts: 18.6 us -> 0.1 us  [on_device(): near_blocks.reshape(-1)]
  transfers between devices with their start and end apart: 16 -> 0, of which waited for: 6 -> 0; matrix products, arithmetic and copies ran while one was open for 28% -> 0% of each run, Pallas kernels for 0% -> 0%
where the time goes in v1:
time: 138 us
  Pallas kernels  131 us (95%)
  local copies, waits for them, and re-layouts  5.58 us (4%)
    pallas_call x1, Pallas kernels, on_device(): pl.pallas_call(functools.partial(planner, ue_count, cell_count), out_shap...  131 us
    unnamed x13, local copies, waits for them, and re-layouts  5.48 us

profile of v1, /device:TPU:0, one launch (start us, length us, event | category | flops | bytes accessed | tf_op | source)
XLA Modules:
  0.0 137.5 jit_solution(16773253453284612169)
XLA Ops:
  0.6 0.8 copy.9
  1.4 0.1 reshape.26.near
  1.5 0.0 copy-start
  1.5 0.7 copy-done
  2.2 0.0 copy-start.1
  2.2 0.7 copy-done.1
  2.9 0.0 copy-start.2
  2.9 0.7 copy-done.2
  3.6 0.0 copy-start.3
  3.6 0.7 copy-done.3
  4.3 0.0 copy-start.4
  4.3 0.7 copy-done.4
  5.0 131.3 %shard_map.86 = (f32[16,1,128]{2,1,0:T(1,128)S(1)}, f32[32,128]{1,0:T(8,128)S(1)}) custom-call(bf16[64,512,128]{2,1,0:T(8,128)(2,1)} %bitcast.11, s32[256]{0:T(256)S(1)} %reshape.26.near, s32[16,1,128]{2,1,0:T(1,128)S(1)} %bitcast.7, s32[16,1,128]{2,1,0:T(1,128)S(1)} %bitcast.8, f32[16,1,128]{2,1,0:T(1,128)S(1)} %bitcast.9, f32[32,128]{1,0:T(8,128)S(1)} %copy-done, ...), custom_call_target="tpu_custom_call" | custom-call | tf_op jit(solution)/shard_map/pallas_call | solution.py:316
  136.3 0.6 copy.12
  136.9 0.6 copy.13
Async XLA Ops:
  1.5 0.7 copy-start
  2.2 0.7 copy-start.1
  2.9 0.7 copy-start.2
  3.6 0.7 copy-start.3
  4.3 0.7 copy-start.4

commit v2 on v1

--- a/solution.py
+++ b/solution.py
@@ -16,12 +16,12 @@
 
 def planner(
     ue_count, cell_count,
-    gains_hbm, near, block_ref, cell_ref, gain_ref, power_ref, avg_ref,
+    gains_hbm, near, block_hbm, cell_hbm, gain_hbm, power_hbm, avg_hbm,
     avg_out, power_out,
-    gains, high, low, power, loads, tails, mine, parts_in, parts_out, terms_in, terms_out,
+    block_ref, cell_ref, gain_ref, gains, high, low, power, loads, tails, mine, parts_in, parts_out, terms_in, terms_out,
     levels, signal_power, log_rates, metrics, spread, pick_cell, put_cell,
     gains_sem, terms_send, terms_recv, parts_send, parts_recv, loads_send, loads_recv,
-    tails_send, tails_recv,
+    tails_send, tails_recv, inputs_sem,
 ):
     device_count = ue_count * cell_count
     ue_at, cell_at = lax.axis_index("ue"), lax.axis_index("cell")
@@ -34,6 +34,17 @@
     def device(number):
         return (number // cell_count, lax.rem(number, cell_count))
 
+    inputs = [
+        pltpu.make_async_copy(source, target, inputs_sem.at[place])
+        for place, (source, target) in enumerate(
+            [
+                (power_hbm, mine), (cell_hbm, cell_ref), (block_hbm, block_ref),
+                (gain_hbm, gain_ref), (avg_hbm, avg_out),
+            ]
+        )
+    ]
+    for copy in inputs:
+        copy.start()
     barrier = pltpu.get_barrier_semaphore()
 
     def greet(step, carry):
@@ -48,8 +59,16 @@
         rows = pl.ds(chunk * home_blocks, home_blocks)
         return pltpu.make_async_copy(gains_hbm.at[rows], gains.at[rows], gains_sem.at[chunk])
 
-    for step in range(1, cell_count + 1):
-        gains_copy(lax.rem(cell_at + step, cell_count)).start()
+    def terms_target(step):
+        chips = cell_count // 2
+        chip = lax.rem(cell_at // 2 + step // 2, chips)
+        return chip * 2 + lax.rem(cell_at + step, 2)
+
+    terms_order = list(range(2, cell_count)) + [1, 0]
+    for step in terms_order:
+        gains_copy(terms_target(step)).start()
+    for copy in inputs:
+        copy.wait()
     pl.semaphore_wait(barrier, device_count - 1)
 
     def spread_copy(table, send_sem, recv_sem, step):
@@ -87,7 +106,7 @@
         )
 
     def terms_copy(step):
-        target = lax.rem(cell_at + step, cell_count)
+        target = terms_target(step)
         return pltpu.make_async_remote_copy(
             src_ref=terms_out.at[step], dst_ref=terms_in.at[step],
             send_sem=terms_send.at[step], recv_sem=terms_recv.at[step],
@@ -100,6 +119,21 @@
             return carry
 
         lax.fori_loop(1, device_count, body, 0)
+
+    def each_near(action):
+        def body(step, carry):
+            action(step * cell_count)
+            return carry
+
+        lax.fori_loop(1, ue_count, body, 0)
+
+    def each_far(action):
+        def body(step, carry):
+            for other in range(1, cell_count):
+                action(step * cell_count + other)
+            return carry
+
+        lax.fori_loop(0, ue_count, body, 0)
 
     def set_power(block, value):
         power[block] = value
@@ -112,9 +146,9 @@
         scale = (0.5 * subbands) / jnp.sum(demand, axis=0, keepdims=True)
         return 0.5 * value + demand * scale
 
-    mine[...] = power_ref[...]
-    split_load(power_ref[...])
-    each_peer(lambda step: spread_copy(*main, step).start())
+    split_load(mine[...])
+    each_near(lambda step: spread_copy(*main, step).start())
+    each_far(lambda step: spread_copy(*main, step).start())
     each_peer(lambda step: spread_copy(*rest, step).start())
     spots = lax.broadcasted_iota(jnp.int32, (width, width), 0)
     for home in range(home_blocks):
@@ -123,15 +157,18 @@
         pick_cell[home // 2, 0:width, columns] = hot.astype(bf16)
         pick_cell[home // 2, width : 2 * width, columns] = hot.astype(bf16)
         put_cell[home * width : (home + 1) * width, :] = hot.T.astype(bf16)
-        avg_out[home] = avg_ref[home]
-    each_peer(lambda step: spread_arrival(*main, step).wait_recv())
-
-    def start_high(block, carry):
+    each_near(lambda step: spread_arrival(*main, step).wait_recv())
+
+    def start_high(index, carry):
+        block = index * cell_count + cell_at
         high[block] = loads[block]
         return carry
 
-    lax.fori_loop(0, device_count, start_high, 0)
-    each_peer(lambda step: spread_copy(*main, step).wait_send())
+    lax.fori_loop(0, ue_count, start_high, 0)
+
+    def finish_loads():
+        each_far(lambda step: spread_arrival(*main, step).wait_recv())
+        each_peer(lambda step: spread_copy(*main, step).wait_send())
 
     def finish_power(turn):
         each_peer(lambda step: spread_arrival(*rest, step).wait_recv())
@@ -164,7 +201,7 @@
                     [high[near[block * near_count + k]] for k in range(near_count)], axis=1
                 )
                 total = jnp.dot(chosen, gains[block], preferred_element_type=f32)
-                if step == cell_count:
+                if step == 0:
                     levels[home] = total
                 else:
                     terms_out[step, home] = total.astype(bf16)
@@ -213,16 +250,18 @@
     piece = 8
 
     def slot(turn, carry):
-        for step in range(1, cell_count + 1):
-            target = lax.rem(cell_at + step, cell_count)
+        for step in terms_order:
+            target = terms_target(step)
 
             @pl.when(turn == 0)
             def _():
                 gains_copy(target).wait()
 
             terms(target, step)
-            if step < cell_count:
+            if step > 0:
                 terms_copy(step).start()
+
+        finish_loads()
 
         @pl.when(turn > 0)
         def _():
@@ -273,29 +312,31 @@
 
         load = lax.fori_loop(1, device_count, add, parts_out[me].astype(f32))
         split_load(load)
-        each_peer(lambda step: spread_copy(*main, step).start())
+        each_near(lambda step: spread_copy(*main, step).start())
+        each_far(lambda step: spread_copy(*main, step).start())
 
         @pl.when(turn < SLOTS - 1)
         def _():
             each_peer(lambda step: spread_copy(*rest, step).start())
 
         mine[...] = next_power(mine[...], load)
-        each_peer(lambda step: parts_copy(lax.rem(me + step, device_count)).wait_send())
-        each_peer(lambda step: spread_arrival(*main, step).wait_recv())
+        each_near(lambda step: spread_arrival(*main, step).wait_recv())
 
         @pl.when(turn < SLOTS - 1)
         def _():
-            def update(block, inner_carry):
+            def update(index, inner_carry):
+                block = index * cell_count + cell_at
                 high[block] = next_power(power[block], loads[block].astype(f32)).astype(bf16)
                 return inner_carry
 
-            lax.fori_loop(0, device_count, update, 0)
+            lax.fori_loop(0, ue_count, update, 0)
             high[me] = mine[...].astype(bf16)
 
-        each_peer(lambda step: spread_copy(*main, step).wait_send())
+        each_peer(lambda step: parts_copy(lax.rem(me + step, device_count)).wait_send())
         return carry
 
     lax.fori_loop(0, SLOTS, slot, 0)
+    finish_loads()
     finish_average()
     power_out[...] = mine[...]
 
@@ -323,9 +364,12 @@
             pl.BlockSpec(memory_space=pl.ANY),
             pl.BlockSpec(memory_space=pltpu.SMEM),
         ]
-        + [in_vmem] * 5,
+        + [pl.BlockSpec(memory_space=pl.ANY)] * 5,
         out_specs=(in_vmem, in_vmem),
         scratch_shapes=[
+            pltpu.VMEM(row, jnp.int32),
+            pltpu.VMEM(row, jnp.int32),
+            pltpu.VMEM(row, f32),
             pltpu.VMEM((blocks, near_count * width, width), bf16),
             pltpu.VMEM(table, bf16),
             pltpu.VMEM(table, bf16),
@@ -353,9 +397,10 @@
             pltpu.SemaphoreType.DMA((device_count,)),
             pltpu.SemaphoreType.DMA((device_count,)),
             pltpu.SemaphoreType.DMA((device_count,)),
+            pltpu.SemaphoreType.DMA((5,)),
         ],
         compiler_params=pltpu.CompilerParams(
-            collective_id=0, has_side_effects=True, vmem_limit_bytes=48 * 1024 * 1024
+            collective_id=0, has_side_effects=True, vmem_limit_bytes=60 * 1024 * 1024
         ),
     )(
         gains.reshape(blocks, near_count * width, width),

time: 138 us -> 126 us (0.913)
  Pallas kernels: 131 us -> 120 us
  local copies, waits for them, and re-layouts: 5.58 us -> 4.06 us
    pallas_call x1, Pallas kernels: 131 us -> 120 us  [on_device(): pl.pallas_call(functools.partial(planner, ue_count, cell_count), out_shap...]
    unnamed x13 -> x3, local copies, waits for them, and re-layouts: 5.48 us -> 3.39 us
where the time goes in v2:
time: 126 us; the launch traced here: 125 us
  Pallas kernels  120 us (95%)
  local copies, waits for them, and re-layouts  4.06 us (3%)
    pallas_call x1, Pallas kernels, on_device(): pl.pallas_call(functools.partial(planner, ue_count, cell_count), out_shap...  120 us
    unnamed x3, local copies, waits for them, and re-layouts  3.39 us

profile of v2, /device:TPU:0, one launch (start us, length us, event | category | flops | bytes accessed | tf_op | source)
XLA Modules:
  0.0 125.2 jit_solution(10766115731759398194)
XLA Ops:
  0.6 0.8 copy.9
  1.4 0.7 reshape.26.near
  2.1 120.5 %shard_map.86 = (f32[16,1,128]{2,1,0:T(1,128)}, f32[32,128]{1,0:T(8,128)}) custom-call(bf16[64,512,128]{2,1,0:T(8,128)(2,1)} %bitcast.6, s32[256]{0:T(256)} %reshape.26.near, s32[16,1,128]{2,1,0:T(1,128)} %bitcast.8, s32[16,1,128]{2,1,0:T(1,128)} %bitcast.9, f32[16,1,128]{2,1,0:T(1,128)} %bitcast.10, f32[32,128]{1,0:T(8,128)} %power_hbm.1, ...), custom_call_target="tpu_custom_call" | custom-call | tf_op jit(solution)/shard_map/pallas_call | solution.py:357
  122.6 1.3 %copy.12 = f32[2048]{0:T(1024)} copy(f32[2048]{0:T(1024)} %bitcast.7) | data formatting | bytes 16384
  123.9 1.3 %copy.13 = f32[32,128]{1,0:T(8,128)} copy(f32[32,128]{1,0:T(8,128)} %get-tuple-element.9) | data formatting | bytes 32768

commit v3 on v2

--- a/solution.py
+++ b/solution.py
@@ -20,8 +20,7 @@
     avg_out, power_out,
     block_ref, cell_ref, gain_ref, gains, high, low, power, loads, tails, mine, parts_in, parts_out, terms_in, terms_out,
     levels, signal_power, log_rates, metrics, spread, pick_cell, put_cell,
-    gains_sem, terms_send, terms_recv, parts_send, parts_recv, loads_send, loads_recv,
-    tails_send, tails_recv, inputs_sem,
+    gains_sem, terms_send, terms_recv, sent, arrived, inputs_sem,
 ):
     device_count = ue_count * cell_count
     ue_at, cell_at = lax.axis_index("ue"), lax.axis_index("cell")
@@ -71,23 +70,28 @@
         copy.wait()
     pl.semaphore_wait(barrier, device_count - 1)
 
-    def spread_copy(table, send_sem, recv_sem, step):
+    near_kind, far_kind, rest_kind, parts_kind = range(4)
+    kind_counts = (
+        ue_count - 1, device_count - ue_count, device_count - 1, device_count - 1
+    )
+
+    def spread_copy(table, kind, step):
         return pltpu.make_async_remote_copy(
             src_ref=table.at[me], dst_ref=table.at[me],
-            send_sem=send_sem.at[step], recv_sem=recv_sem.at[step],
+            send_sem=sent.at[kind], recv_sem=arrived.at[kind],
             device_id=device(lax.rem(me + step, device_count)), device_id_type=MESH,
         )
 
-    def spread_arrival(table, send_sem, recv_sem, step):
-        source = lax.rem(me - step + device_count, device_count)
-        return pltpu.make_async_remote_copy(
-            src_ref=table.at[source], dst_ref=table.at[source],
-            send_sem=send_sem.at[step], recv_sem=recv_sem.at[step],
-            device_id=device(source), device_id_type=MESH,
-        )
-
-    main = (loads, loads_send, loads_recv)
-    rest = (tails, tails_send, tails_recv)
+    def wait_all(semaphores, table, kind):
+        rows = table.at[pl.ds(0, kind_counts[kind])]
+        pltpu.make_async_copy(rows, rows, semaphores.at[kind]).wait()
+
+    def send_loads():
+        each_near(lambda step: spread_copy(loads, near_kind, step).start())
+        each_far(lambda step: spread_copy(loads, far_kind, step).start())
+
+    def send_tails():
+        each_peer(lambda step: spread_copy(tails, rest_kind, step).start())
 
     def split_load(value):
         top = value.astype(bf16)
@@ -101,7 +105,7 @@
         step = lax.rem(owner - me + device_count, device_count)
         return pltpu.make_async_remote_copy(
             src_ref=parts_out.at[owner], dst_ref=parts_in.at[step],
-            send_sem=parts_send.at[step], recv_sem=parts_recv.at[step],
+            send_sem=sent.at[parts_kind], recv_sem=arrived.at[parts_kind],
             device_id=device(owner), device_id_type=MESH,
         )
 
@@ -147,9 +151,8 @@
         return 0.5 * value + demand * scale
 
     split_load(mine[...])
-    each_near(lambda step: spread_copy(*main, step).start())
-    each_far(lambda step: spread_copy(*main, step).start())
-    each_peer(lambda step: spread_copy(*rest, step).start())
+    send_loads()
+    send_tails()
     spots = lax.broadcasted_iota(jnp.int32, (width, width), 0)
     for home in range(home_blocks):
         hot = (spots == cell_ref[home]).astype(f32)
@@ -157,7 +160,7 @@
         pick_cell[home // 2, 0:width, columns] = hot.astype(bf16)
         pick_cell[home // 2, width : 2 * width, columns] = hot.astype(bf16)
         put_cell[home * width : (home + 1) * width, :] = hot.T.astype(bf16)
-    each_near(lambda step: spread_arrival(*main, step).wait_recv())
+    wait_all(arrived, loads, near_kind)
 
     def start_high(index, carry):
         block = index * cell_count + cell_at
@@ -167,11 +170,12 @@
     lax.fori_loop(0, ue_count, start_high, 0)
 
     def finish_loads():
-        each_far(lambda step: spread_arrival(*main, step).wait_recv())
-        each_peer(lambda step: spread_copy(*main, step).wait_send())
+        wait_all(arrived, loads, far_kind)
+        wait_all(sent, loads, far_kind)
+        wait_all(sent, loads, near_kind)
 
     def finish_power(turn):
-        each_peer(lambda step: spread_arrival(*rest, step).wait_recv())
+        wait_all(arrived, tails, rest_kind)
 
         @pl.when(turn == 0)
         def _():
@@ -190,12 +194,12 @@
             lax.fori_loop(0, device_count, later, 0)
 
         set_power(me, mine[...])
-        each_peer(lambda step: spread_copy(*rest, step).wait_send())
+        wait_all(sent, tails, rest_kind)
 
     def terms(target, step):
         def body(group, carry):
-            for inner in range(4):
-                home = group * 4 + inner
+            for inner in range(8):
+                home = group * 8 + inner
                 block = target * home_blocks + home
                 chosen = jnp.concatenate(
                     [high[near[block * near_count + k]] for k in range(near_count)], axis=1
@@ -207,7 +211,7 @@
                     terms_out[step, home] = total.astype(bf16)
             return carry
 
-        lax.fori_loop(0, home_blocks // 4, body, 0)
+        lax.fori_loop(0, home_blocks // 8, body, 0)
 
     group_blocks = 16
 
@@ -306,21 +310,19 @@
         for step in range(1, cell_count):
             terms_copy(step).wait_send()
 
-        def add(step, total):
-            parts_copy(lax.rem(me + step, device_count)).wait_recv()
-            return total + parts_in[step].astype(f32)
-
-        load = lax.fori_loop(1, device_count, add, parts_out[me].astype(f32))
+        wait_all(arrived, parts_in, parts_kind)
+        load = parts_out[me].astype(f32)
+        for step in range(1, device_count):
+            load = load + parts_in[step].astype(f32)
         split_load(load)
-        each_near(lambda step: spread_copy(*main, step).start())
-        each_far(lambda step: spread_copy(*main, step).start())
+        send_loads()
 
         @pl.when(turn < SLOTS - 1)
         def _():
-            each_peer(lambda step: spread_copy(*rest, step).start())
+            send_tails()
 
         mine[...] = next_power(mine[...], load)
-        each_near(lambda step: spread_arrival(*main, step).wait_recv())
+        wait_all(arrived, loads, near_kind)
 
         @pl.when(turn < SLOTS - 1)
         def _():
@@ -332,7 +334,7 @@
             lax.fori_loop(0, ue_count, update, 0)
             high[me] = mine[...].astype(bf16)
 
-        each_peer(lambda step: parts_copy(lax.rem(me + step, device_count)).wait_send())
+        wait_all(sent, parts_out, parts_kind)
         return carry
 
     lax.fori_loop(0, SLOTS, slot, 0)
@@ -391,12 +393,8 @@
             pltpu.SemaphoreType.DMA((cell_count,)),
             pltpu.SemaphoreType.DMA((cell_count,)),
             pltpu.SemaphoreType.DMA((cell_count,)),
-            pltpu.SemaphoreType.DMA((device_count,)),
-            pltpu.SemaphoreType.DMA((device_count,)),
-            pltpu.SemaphoreType.DMA((device_count,)),
-            pltpu.SemaphoreType.DMA((device_count,)),
-            pltpu.SemaphoreType.DMA((device_count,)),
-            pltpu.SemaphoreType.DMA((device_count,)),
+            pltpu.SemaphoreType.DMA((4,)),
+            pltpu.SemaphoreType.DMA((4,)),
             pltpu.SemaphoreType.DMA((5,)),
         ],
         compiler_params=pltpu.CompilerParams(

time: 126 us -> 122 us (0.968)
  Pallas kernels: 120 us -> 117 us
    pallas_call x1, Pallas kernels: 120 us -> 117 us  [on_device(): pl.pallas_call(functools.partial(planner, ue_count, cell_count), out_shap...]
where the time goes in v3:
time: 122 us
  Pallas kernels  117 us (96%)
  local copies, waits for them, and re-layouts  4.06 us (3%)
    pallas_call x1, Pallas kernels, on_device(): pl.pallas_call(functools.partial(planner, ue_count, cell_count), out_shap...  117 us
    unnamed x3, local copies, waits for them, and re-layouts  3.39 us

profile of v3, /device:TPU:0, one launch (start us, length us, event | category | flops | bytes accessed | tf_op | source)
XLA Modules:
  0.0 121.8 jit_solution(15807410465804874431)
XLA Ops:
  0.6 0.8 copy.9
  1.4 0.7 reshape.26.near
  2.1 117.1 %shard_map.86 = (f32[16,1,128]{2,1,0:T(1,128)}, f32[32,128]{1,0:T(8,128)}) custom-call(bf16[64,512,128]{2,1,0:T(8,128)(2,1)} %bitcast.6, s32[256]{0:T(256)} %reshape.26.near, s32[16,1,128]{2,1,0:T(1,128)} %bitcast.8, s32[16,1,128]{2,1,0:T(1,128)} %bitcast.9, f32[16,1,128]{2,1,0:T(1,128)} %bitcast.10, f32[32,128]{1,0:T(8,128)} %power_hbm.1, ...), custom_call_target="tpu_custom_call" | custom-call | tf_op jit(solution)/shard_map/pallas_call | solution.py:359
  119.1 1.3 %copy.12 = f32[2048]{0:T(1024)} copy(f32[2048]{0:T(1024)} %bitcast.7) | data formatting | bytes 16384
  120.4 1.3 %copy.13 = f32[32,128]{1,0:T(8,128)} copy(f32[32,128]{1,0:T(8,128)} %get-tuple-element.9) | data formatting | bytes 32768

commit v4 on v3

--- a/solution.py
+++ b/solution.py
@@ -139,6 +139,14 @@
 
         lax.fori_loop(0, ue_count, body, 0)
 
+    def each_block(count, action):
+        def body(group, carry):
+            for inner in range(4):
+                action(group * 4 + inner)
+            return carry
+
+        lax.fori_loop(0, count // 4, body, 0)
+
     def set_power(block, value):
         power[block] = value
         top = value.astype(bf16)
@@ -179,27 +187,22 @@
 
         @pl.when(turn == 0)
         def _():
-            def first(block, carry):
-                set_power(block, whole_load(block))
-                return carry
-
-            lax.fori_loop(0, device_count, first, 0)
+            each_block(device_count, lambda block: set_power(block, whole_load(block)))
 
         @pl.when(turn > 0)
         def _():
-            def later(block, carry):
+            def later(block):
                 set_power(block, next_power(power[block], whole_load(block)))
-                return carry
-
-            lax.fori_loop(0, device_count, later, 0)
+
+            each_block(device_count, later)
 
         set_power(me, mine[...])
         wait_all(sent, tails, rest_kind)
 
     def terms(target, step):
         def body(group, carry):
-            for inner in range(8):
-                home = group * 8 + inner
+            for inner in range(16):
+                home = group * 16 + inner
                 block = target * home_blocks + home
                 chosen = jnp.concatenate(
                     [high[near[block * near_count + k]] for k in range(near_count)], axis=1
@@ -211,12 +214,12 @@
                     terms_out[step, home] = total.astype(bf16)
             return carry
 
-        lax.fori_loop(0, home_blocks // 8, body, 0)
+        lax.fori_loop(0, home_blocks // 16, body, 0)
 
     group_blocks = 16
 
     def gather(table, result):
-        def body(pair, carry):
+        def one(pair):
             names = jnp.concatenate([block_ref[2 * pair], block_ref[2 * pair + 1]], axis=1)
             total = jnp.zeros((subbands, 2 * width), f32)
             for first in range(0, device_count, group_blocks):
@@ -232,9 +235,8 @@
                     )
             result[2 * pair] = total[:, :width]
             result[2 * pair + 1] = total[:, width:]
-            return carry
-
-        lax.fori_loop(0, pairs, body, 0)
+
+        each_block(pairs, one)
 
     def power_rows(first):
         rows = slice(first, first + group_blocks)
@@ -326,12 +328,11 @@
 
         @pl.when(turn < SLOTS - 1)
         def _():
-            def update(index, inner_carry):
+            def update(index):
                 block = index * cell_count + cell_at
                 high[block] = next_power(power[block], loads[block].astype(f32)).astype(bf16)
-                return inner_carry
-
-            lax.fori_loop(0, ue_count, update, 0)
+
+            each_block(ue_count, update)
             high[me] = mine[...].astype(bf16)
 
         wait_all(sent, parts_out, parts_kind)

time: 122 us -> 116 us (0.951)
  Pallas kernels: 117 us -> 110 us
    pallas_call x1, Pallas kernels: 117 us -> 110 us  [on_device(): pl.pallas_call(functools.partial(planner, ue_count, cell_count), out_shap...]
where the time goes in v4:
time: 116 us; the launch traced here: 115 us
  Pallas kernels  110 us (95%)
  local copies, waits for them, and re-layouts  4.06 us (3%)
    pallas_call x1, Pallas kernels, on_device(): pl.pallas_call(functools.partial(planner, ue_count, cell_count), out_shap...  110 us
    unnamed x3, local copies, waits for them, and re-layouts  3.39 us

profile of v4, /device:TPU:0, one launch (start us, length us, event | category | flops | bytes accessed | tf_op | source)
XLA Modules:
  0.0 115.1 jit_solution(17487494154330770699)
XLA Ops:
  0.6 0.8 copy.9
  1.4 0.7 reshape.26.near
  2.1 110.4 %shard_map.86 = (f32[16,1,128]{2,1,0:T(1,128)}, f32[32,128]{1,0:T(8,128)}) custom-call(bf16[64,512,128]{2,1,0:T(8,128)(2,1)} %bitcast.6, s32[256]{0:T(256)} %reshape.26.near, s32[16,1,128]{2,1,0:T(1,128)} %bitcast.8, s32[16,1,128]{2,1,0:T(1,128)} %bitcast.9, f32[16,1,128]{2,1,0:T(1,128)} %bitcast.10, f32[32,128]{1,0:T(8,128)} %power_hbm.1, ...), custom_call_target="tpu_custom_call" | custom-call | tf_op jit(solution)/shard_map/pallas_call | solution.py:360
  112.5 1.3 %copy.12 = f32[2048]{0:T(1024)} copy(f32[2048]{0:T(1024)} %bitcast.7) | data formatting | bytes 16384
  113.8 1.3 %copy.13 = f32[32,128]{1,0:T(8,128)} copy(f32[32,128]{1,0:T(8,128)} %get-tuple-element.9) | data formatting | bytes 32768

commit v5 on v4

--- a/solution.py
+++ b/solution.py
@@ -125,11 +125,8 @@
         lax.fori_loop(1, device_count, body, 0)
 
     def each_near(action):
-        def body(step, carry):
+        for step in range(1, ue_count):
             action(step * cell_count)
-            return carry
-
-        lax.fori_loop(1, ue_count, body, 0)
 
     def each_far(action):
         def body(step, carry):
@@ -308,7 +305,10 @@
 
             return inner_carry
 
-        lax.fori_loop(0, device_count // piece, scatter, 0)
+        def scatter_two(group, inner_carry):
+            return scatter(2 * group + 1, scatter(2 * group, inner_carry))
+
+        lax.fori_loop(0, device_count // piece // 2, scatter_two, 0)
         for step in range(1, cell_count):
             terms_copy(step).wait_send()
 

time: 116 us -> 115 us (level)
  no operation moved by 1% of the time
where the time goes in v5:
time: 115 us
  Pallas kernels  110 us (96%)
  local copies, waits for them, and re-layouts  4.06 us (4%)
    pallas_call x1, Pallas kernels, on_device(): pl.pallas_call(functools.partial(planner, ue_count, cell_count), out_shap...  110 us
    unnamed x3, local copies, waits for them, and re-layouts  3.39 us

profile of v5, /device:TPU:0, one launch (start us, length us, event | category | flops | bytes accessed | tf_op | source)
XLA Modules:
  0.0 115.0 jit_solution(1731513944978981338)
XLA Ops:
  0.6 0.8 copy.9
  1.4 0.7 reshape.26.near
  2.1 110.3 %shard_map.86 = (f32[16,1,128]{2,1,0:T(1,128)}, f32[32,128]{1,0:T(8,128)}) custom-call(bf16[64,512,128]{2,1,0:T(8,128)(2,1)} %bitcast.6, s32[256]{0:T(256)} %reshape.26.near, s32[16,1,128]{2,1,0:T(1,128)} %bitcast.8, s32[16,1,128]{2,1,0:T(1,128)} %bitcast.9, f32[16,1,128]{2,1,0:T(1,128)} %bitcast.10, f32[32,128]{1,0:T(8,128)} %power_hbm.1, ...), custom_call_target="tpu_custom_call" | custom-call | tf_op jit(solution)/shard_map/pallas_call | solution.py:360
  112.4 1.3 %copy.12 = f32[2048]{0:T(1024)} copy(f32[2048]{0:T(1024)} %bitcast.7) | data formatting | bytes 16384
  113.7 1.3 %copy.13 = f32[32,128]{1,0:T(8,128)} copy(f32[32,128]{1,0:T(8,128)} %get-tuple-element.9) | data formatting | bytes 32768
